TPU v7x, 256 devices: a whole 4x4x8 slice. The times are simulated.
256 devices in a mesh: dp: 32 (over z, x_hi, core), tensor: 8 (over x_lo, y).
Axes of the slice: x: 4 (x_hi: 2, x_lo: 2; x = x_hi * 2 + x_lo), y: 4, z: 8, core: 2. Of those that a mesh axis runs over, the one named last changes fastest.
Arguments:
- tokens: bfloat16 [16384, 3072], P('dp', 'tensor'), may hold values from -6 to 6
- hidden_cot: bfloat16 [16384, 8192], P('dp', 'tensor'), may hold values from -1.5 to 1.5
- w_gate: bfloat16 [3072, 8192], P(None, 'tensor'), may hold values from -0.109375 to 0.109375
- w_up: bfloat16 [3072, 8192], P(None, 'tensor'), may hold values from -0.109375 to 0.109375
- expert_ids: int32 [16384, 2], P('dp'), may hold values from 0 to 7, as said below
- route_fixed: int32 [16384, 2], P('dp'), may hold values from 4096 to 65535
Outputs:
- token_grad: bfloat16 [16384, 3072], P('dp', 'tensor')
- gate_grad: bfloat16 [3072, 8192], P('dp', 'tensor')
- up_grad: bfloat16 [3072, 8192], P('dp', 'tensor')
- route_grad: float32 [16384], P('dp')
Inputs may be any that keep to these rules, and one draw needn't show every extreme that they name: `expert_ids`: each row names 2 different experts; in each aligned block of 512 rows (the rows of one index of dp), between 128 and 256 rows name expert 0, and exactly 256 in some block.
All inputs are finite; a program needn't handle non-finite values.
Results may differ from a plain program's by a relative error of at most 0.0049.
Values may be sent and summed in bfloat16 or wider, within the bound.
No kernel may reach another device: no remote copies, remote signals or barrier semaphores. Data moves between devices by JAX's collectives and lax.ppermute only.
A program may use at most 128 MiB of HBM per device.

v0:
```python
import jax
import jax.numpy as jnp
from jax import lax
from jax.sharding import PartitionSpec as P

CAP = 256


def on_device(tokens, hidden_cot, w_gate, w_up, expert_ids, route_fixed):
    selected = expert_ids == 0
    routed_flag = jnp.any(selected, axis=1)
    slot_of = jnp.cumsum(routed_flag.astype(jnp.int32)) - 1
    slot_ids = jnp.arange(CAP, dtype=jnp.int32)
    dispatch_mask = (slot_of[None, :] == slot_ids[:, None]) & routed_flag[None, :]
    dispatch = dispatch_mask.astype(jnp.bfloat16)
    dispatch_wide = dispatch_mask.astype(jnp.float32)
    share_all = jnp.sum(jnp.where(selected, route_fixed, 0), axis=1).astype(jnp.float32) / 65536.0
    share = jnp.dot(dispatch_wide, share_all, precision=lax.Precision.HIGHEST)
    routed = jnp.sum(dispatch_wide, axis=1)
    picked = jnp.dot(dispatch, tokens, preferred_element_type=jnp.float32).astype(jnp.bfloat16)
    cot_rows = jnp.dot(dispatch, hidden_cot, preferred_element_type=jnp.float32).astype(
        jnp.bfloat16
    )
    gathered = lax.all_gather(picked, "tensor", axis=1, tiled=True)
    gate_pre = jnp.dot(gathered, w_gate, preferred_element_type=jnp.float32)
    up_pre = jnp.dot(gathered, w_up, preferred_element_type=jnp.float32)
    sigmoid_gate = jax.nn.sigmoid(gate_pre)
    activated = gate_pre * sigmoid_gate
    hidden = (activated * up_pre).astype(jnp.bfloat16)
    hidden = lax.optimization_barrier(hidden)
    hidden_wide = hidden.astype(jnp.float32)
    cot_wide = cot_rows.astype(jnp.float32)
    slot_route = routed * lax.psum(jnp.sum(hidden_wide * cot_wide, axis=1), "tensor")
    route_grad = jnp.dot(slot_route, dispatch_wide, precision=lax.Precision.HIGHEST)
    scaled = share[:, None] * cot_wide
    gate_cot = (scaled * up_pre * sigmoid_gate * (1.0 + gate_pre * (1.0 - sigmoid_gate))).astype(
        jnp.bfloat16
    )
    up_cot = (scaled * activated).astype(jnp.bfloat16)
    hidden_width = w_gate.shape[1]
    dims = (((1,), (1,)), ((), ()))
    first = lax.dot_general(w_gate, gate_cot, dims, preferred_element_type=jnp.float32)
    transposed = lax.psum_scatter(
        first + lax.dot_general(w_up, up_cot, dims, preferred_element_type=jnp.float32),
        "tensor",
        scatter_dimension=0,
        tiled=True,
    )
    slot_grad = transposed.T.astype(jnp.bfloat16)
    back_dims = (((0,), (0,)), ((), ()))
    token_grad = lax.dot_general(
        dispatch, slot_grad, back_dims, preferred_element_type=jnp.float32
    ).astype(jnp.bfloat16)
    rows_dims = (((0,), (0,)), ((), ()))
    stacked_cot = jnp.concatenate([gate_cot, up_cot], axis=1)
    summed = lax.psum_scatter(
        lax.dot_general(gathered, stacked_cot, rows_dims, preferred_element_type=jnp.float32),
        "dp",
        scatter_dimension=0,
        tiled=True,
    )
    gate_grad = summed[:, :hidden_width]
    up_grad = summed[:, hidden_width:]
    return (token_grad, gate_grad.astype(jnp.bfloat16), up_grad.astype(jnp.bfloat16), route_grad)


def solution(mesh):
    return jax.shard_map(
        on_device,
        mesh=mesh,
        in_specs=(
            P("dp", "tensor"),
            P("dp", "tensor"),
            P(None, "tensor"),
            P(None, "tensor"),
            P("dp", None),
            P("dp", None),
        ),
        out_specs=(P("dp", "tensor"), P("dp", "tensor"), P("dp", "tensor"), P("dp")),
        check_vma=False,
    )
```

profile of v0, /device:TPU:2, one launch (start us, length us, event | category | flops | bytes accessed | tf_op | source)
XLA Modules:
  0.0 403.8 jit_solution(13481215032266457970)
XLA Ops:
  7.2 0.0 copy-start
  7.2 0.0 all-gather.2.cloned.1.call-start
  7.2 0.8 fusion.32
  8.0 0.3 reduce-window.9
  8.3 0.1 slice.15
  8.4 0.1 slice_reduce_fusion
  8.6 0.1 add_bitcast_fusion
  8.6 2.0 convolution_convert_fusion.2
  10.6 0.0 all-gather.2.cloned.1.call-update
  10.6 0.0 reduce-scatter.3.cloned.1.call-start
  10.7 0.7 select_reduce_fusion
  11.4 0.3 fusion.19
  11.8 0.0 copy-done
  11.8 1.3 convolution_convert_fusion
  13.0 42.7 %all-gather.2.cloned.1.call-done = bf16[256,3072]{1,0:T(8,128)(2,1)} async-done(((bf16[256,384]{1,0:T(8,128)(2,1)}), bf16[256,3072]{1,0:T(8,128)(2,1)}) %all-gather.2.cloned.1.call-update) | async-done | bytes 1572880 | tf_op jit(solution)/shard_map/all_gather | solution.py:24
  55.8 0.0 copy-start.1
  55.8 0.0 copy-start.3
  55.8 0.0 slice-start.2
  55.8 0.0 slice-start
  55.8 5.2 %fusion.35 = f32[256,1024]{1,0:T(8,128)S(1)} fusion(bf16[256,3072]{1,0:T(8,128)(2,1)} %all-gather.2.cloned.1.call-done, bf16[3072,1024]{1,0:T(8,128)(2,1)} %param.8), kind=kOutput, calls=%fused_computation.46 | convolution fusion | flops 1610612736 | bytes 8912896 | tf_op jit(solution)/shard_map/dot_general | solution.py:25
  61.0 0.0 copy-done.1
  61.0 0.0 copy-done.3
  61.0 0.0 slice-start.3
  61.0 0.0 slice-start.1
  61.0 5.9 %multiply_convert_fusion = (bf16[256,1024]{1,0:T(8,128)(2,1)}, bf16[256,1024]{1,0:T(8,128)(2,1)S(1)}, bf16[256,1024]{1,0:T(8,128)(2,1)S(1)}) fusion(f32[256,1024]{1,0:T(8,128)S(1)} %fusion.35, bf16[256,1024]{1,0:T(8,128)(2,1)S(1)} %copy-done.3, f32[256]{0:T(256)S(1)} %bitcast.30, bf16[256,3072]{1,0:T(8,128)(2,1)S(1)} %copy-done.1, bf16[3072,1024]{1,0:T(8,128)(2,1)} %param.9), kind=kOutput, calls=%fused_computation.18 | convolution fusion | flops 1615069184 | bytes 11011072 | tf_op jit(solution)/shard_map/dot_general | solution.py:26
  67.0 0.0 copy-start.2
  67.0 0.0 slice-done.2
  67.0 0.0 slice-done.3
  67.0 1.9 fusion.36
  68.9 0.0 copy-done.2
  68.9 0.0 slice-done
  68.9 0.0 slice-done.1
  68.9 3.6 fusion
  72.5 0.0 reduce-scatter.3.cloned.1.call-update
  72.5 0.0 reduce-scatter.5.cloned.1.call-start
  72.6 11.2 %fusion.8 = f32[3072,2048]{1,0:T(8,128)} fusion(bf16[256,3072]{1,0:T(8,128)(2,1)S(1)} %copy-done.1, bf16[256,1024]{1,0:T(8,128)(2,1)S(1)} %get-tuple-element.6, bf16[256,1024]{1,0:T(8,128)(2,1)} %copy-done.2), kind=kOutput, calls=%fused_computation.14 | convolution fusion | flops 3223322624 | bytes 27787264 | tf_op jit(solution)/shard_map/dot_general | solution.py:57
  83.8 0.0 reduce-scatter.5.cloned.1.call-update
  83.8 0.2 convert_reduce_fusion
  84.0 0.9 copy-done.4
  84.9 0.2 copy-done.5
  85.1 0.2 fusion.7
  85.3 17.2 %psum.7 = f32[256]{0:T(256)S(1)} all-reduce(f32[256]{0:T(256)S(1)} %fusion.7), channel_id=1, replica_groups=mesh['dp'=32,'tensor'=8] {'tensor'}, use_global_device_ids=true, to_apply=%region_8.9 | all-reduce | flops 256 | bytes 2048 | tf_op jit(solution)/shard_map/psum | solution.py:33
  102.5 0.9 fusion.14
  103.3 17.2 %reduce-scatter.3.cloned.1.call-done = f32[384,256]{0,1:T(8,128)} async-done(((f32[3072,256]{0,1:T(8,128)}), f32[384,256]{0,1:T(8,128)}) %reduce-scatter.3.cloned.1.call-update) | async-done | bytes 393232 | tf_op jit(solution)/shard_map/reduce_scatter | solution.py:43
  120.6 2.1 convolution_convert_fusion.1
  122.7 272.7 %reduce-scatter.5.cloned.1.call-done = f32[96,2048]{1,0:T(8,128)} async-done(((f32[3072,2048]{1,0:T(8,128)}), f32[96,2048]{1,0:T(8,128)}) %reduce-scatter.5.cloned.1.call-update) | async-done | bytes 786448 | tf_op jit(solution)/shard_map/reduce_scatter | solution.py:56
  395.3 1.2 convert.5
  396.5 0.8 fusion.34
  (8 shorter events, 0.1 us)
Async XLA Ops:
  7.2 4.6 %copy-start = (bf16[512,1024]{1,0:T(8,128)(2,1)S(1)}, bf16[512,1024]{1,0:T(8,128)(2,1)}, u32[]{:S(2)}) copy-start(bf16[512,1024]{1,0:T(8,128)(2,1)} %param.7) | copy-start | bytes 3145732
  7.2 48.6 %all-gather.2.cloned.1.call-start = ((), (), s32[]{:S(2)}) async-start(), calls=%async_computation.2 | async-start | bytes 1769472 | tf_op jit(solution)/shard_map/all_gather | solution.py:24
  10.6 109.9 %reduce-scatter.3.cloned.1.call-start = ((), (), s32[]{:S(2)}) async-start(), calls=%async_computation.3 | async-start | bytes 3538944 | tf_op jit(solution)/shard_map/reduce_scatter | solution.py:43
  55.8 5.2 %copy-start.1 = (bf16[256,3072]{1,0:T(8,128)(2,1)S(1)}, bf16[256,3072]{1,0:T(8,128)(2,1)}, u32[]{:S(2)}) copy-start(bf16[256,3072]{1,0:T(8,128)(2,1)} %all-gather.2.cloned.1.call-done) | copy-start | bytes 4718596
  55.8 5.2 %copy-start.3 = (bf16[256,1024]{1,0:T(8,128)(2,1)S(1)}, bf16[256,1024]{1,0:T(8,128)(2,1)}, u32[]{:S(2)}) copy-start(bf16[256,1024]{1,0:T(8,128)(2,1)} %convolution_convert_fusion) | copy-start | bytes 1572868
  55.8 11.2 %slice-start.2 = ((s8[6291456]{0:T(1024)(128)(4,1)}), s8[4194304]{0:T(1024)(128)(4,1)S(1)}, s32[]{:S(2)}) async-start(s8[6291456]{0:T(1024)(128)(4,1)} %bitcast.27), calls=%async_computation.7 | async-start | bytes 8388608
  55.8 13.1 %slice-start = ((s8[6291456]{0:T(1024)(128)(4,1)}), s8[4194304]{0:T(1024)(128)(4,1)S(1)}, s32[]{:S(2)}) async-start(s8[6291456]{0:T(1024)(128)(4,1)} %bitcast.23), calls=%async_computation.5 | async-start | bytes 8388608
  61.0 6.0 %slice-start.3 = ((s8[6291456]{0:T(1024)(128)(4,1)}), s8[2097152]{0:T(1024)(128)(4,1)S(1)}, s32[]{:S(2)}) async-start(s8[6291456]{0:T(1024)(128)(4,1)} %bitcast.27), calls=%async_computation.8 | async-start | bytes 4194304
  61.0 7.9 %slice-start.1 = ((s8[6291456]{0:T(1024)(128)(4,1)}), s8[2097152]{0:T(1024)(128)(4,1)S(1)}, s32[]{:S(2)}) async-start(s8[6291456]{0:T(1024)(128)(4,1)} %bitcast.23), calls=%async_computation.6 | async-start | bytes 4194304
  67.0 1.9 copy-start.2
  72.5 322.8 %reduce-scatter.5.cloned.1.call-start = ((), (), s32[]{:S(2)}) async-start(), calls=%async_computation.4 | async-start | bytes 25952256 | tf_op jit(solution)/shard_map/reduce_scatter | solution.py:56
  83.8 1.1 copy-start.4
  83.8 1.3 copy-start.5
Sparse Core Ops, SparseCore 0:
  10.8 44.9 all-gather.1
  72.7 47.8 reduce-scatter.2
  125.2 270.0 reduce-scatter.4
where the time goes:
time: 405 us; the launch traced here: 404 us
  waiting for transfers between devices  333 us (82%)
  matrix products  34.4 us (8%)
  blocking collectives  17.2 us (4%)
  between operations  13.9 us (3%)
    reduce_scatter x1, waiting for transfers between devices, on_device(): lax.psum_scatter(lax.dot_general(gathered, stacked_cot, rows_dims, prefer...  273 us
    all_gather x1, waiting for transfers between devices, on_device(): gathered = lax.all_gather(picked, 'tensor', axis=1, tiled=True)  42.7 us
    reduce_scatter x1, waiting for transfers between devices, on_device(): lax.psum_scatter(first + lax.dot_general(w_up, up_cot, dims, preferred_el...  17.2 us
    psum x1, blocking collectives, on_device(): lax.psum(jnp.sum(hidden_wide * cot_wide, axis=1), 'tensor')  17.2 us
    dot_general x1, matrix products, on_device(): lax.dot_general(gathered, stacked_cot, rows_dims, preferred_element_type=...  11.2 us
  transfers between devices with their start and end apart: 3, of which 3 were waited for; matrix products, arithmetic and copies ran while one was open for 4% of the time, Pallas kernels for 0%

commit v1 on v0

v1 whole, which is shorter than its diff:
```python
import jax
import jax.numpy as jnp
from jax import lax
from jax.sharding import PartitionSpec as P

CAP = 256
BF = jnp.bfloat16
F32 = jnp.float32


def on_device(tokens, hidden_cot, w_gate, w_up, expert_ids, route_fixed):
    tok_dev, piece = tokens.shape
    width = w_gate.shape[1]
    n_tensor = lax.axis_size("tensor")
    n_dp = lax.axis_size("dp")
    n_z = n_dp // 4
    rows = piece // 4
    t = lax.axis_index("tensor")
    dp = lax.axis_index("dp")
    xh, core = (dp // 2) % 2, dp % 2

    def over_tensor(x, k):
        return lax.ppermute(x, "tensor", [(i, i ^ k) for i in range(n_tensor)])

    def over_dp(x, k):
        return lax.ppermute(x, "dp", [(i, i ^ k) for i in range(n_dp)])

    selected = expert_ids == 0
    flag = jnp.any(selected, axis=1)
    place = jnp.arange(tok_dev, dtype=jnp.int32)
    upto = (place[:, None] <= place[None, :]).astype(BF)
    slot_of = jnp.dot(flag.astype(BF)[None, :], upto, preferred_element_type=F32)[0] - 1.0
    slot_of = jnp.where(flag, slot_of.astype(jnp.int32), -1)
    mask = slot_of[None, :] == jnp.arange(CAP, dtype=jnp.int32)[:, None]
    dispatch = mask.astype(BF)
    share_all = jnp.sum(jnp.where(selected, route_fixed, 0), axis=1).astype(F32) / 65536.0
    share = jnp.sum(jnp.where(mask, share_all[None, :], 0.0), axis=1)

    picked = lax.dot_general(
        tokens, dispatch, (((0,), (1,)), ((), ())), preferred_element_type=F32
    ).astype(BF)
    far_piece = over_dp(
        lax.dynamic_slice_in_dim(picked, (1 - xh) * 2 * rows, 2 * rows, 0), 2
    )
    near = jnp.zeros((n_tensor, piece, CAP), BF)
    for k in range(n_tensor):
        got = over_tensor(picked, k) if k else picked
        near = lax.dynamic_update_index_in_dim(near, got, t ^ k, 0)
    cot_rows = jnp.dot(dispatch, hidden_cot, preferred_element_type=F32).astype(BF)

    gathered = near.reshape(n_tensor * piece, CAP)
    first = (((0,), (0,)), ((), ()))
    gate_pre = lax.dot_general(gathered, w_gate, first, preferred_element_type=F32)
    up_pre = lax.dot_general(gathered, w_up, first, preferred_element_type=F32)
    sig = jax.nn.sigmoid(gate_pre)
    activated = gate_pre * sig
    hidden = lax.optimization_barrier((activated * up_pre).astype(BF))
    cot_wide = cot_rows.astype(F32)
    route_part = jnp.sum(hidden.astype(F32) * cot_wide, axis=1)
    scaled = share[:, None] * cot_wide
    gate_cot = (scaled * up_pre * sig * (1.0 + gate_pre * (1.0 - sig))).astype(BF)
    up_cot = (scaled * activated).astype(BF)

    far = jnp.zeros((n_tensor, 2 * rows, CAP), BF)
    for k in range(n_tensor):
        got = over_tensor(far_piece, k) if k else far_piece
        far = lax.dynamic_update_index_in_dim(far, got, t ^ k, 0)
    near4 = near.reshape(n_tensor, 4, rows, CAP)
    far2 = far.reshape(n_tensor, 2, rows, CAP)
    mine = lambda a, i: lax.dynamic_index_in_dim(a, i, 1, keepdims=False)
    own_rows = mine(near4, xh * 2 + core)
    own_far = mine(far2, core)
    sib_rows = over_dp(mine(near4, xh * 2 + 1 - core), 1)
    sib_far = over_dp(mine(far2, 1 - core), 1)
    left = jnp.concatenate([own_rows, sib_rows, own_far, sib_far], axis=2)
    left = left.reshape(n_tensor * rows, 4 * CAP)

    cots = jnp.concatenate([gate_cot, up_cot], axis=1)
    far_cots = over_dp(cots, 2)
    sib_cots = over_dp(cots, 1)
    sib_far_cots = over_dp(far_cots, 1)
    right = jnp.concatenate([cots, sib_cots, far_cots, sib_far_cots], axis=0)
    part = jnp.dot(left, right, preferred_element_type=F32).astype(BF)
    groups = [[4 * z + q for z in range(n_z)] for q in range(4)]
    summed = lax.psum_scatter(
        part, "dp", scatter_dimension=0, tiled=True, axis_index_groups=groups
    )

    last = (((1,), (1,)), ((), ()))
    total = jnp.zeros((CAP, piece), F32)
    for k in range(n_tensor):
        wg = lax.dynamic_slice_in_dim(w_gate, (t ^ k) * piece, piece, 0)
        wu = lax.dynamic_slice_in_dim(w_up, (t ^ k) * piece, piece, 0)
        out = lax.dot_general(gate_cot, wg, last, preferred_element_type=F32)
        out = out + lax.dot_general(up_cot, wu, last, preferred_element_type=F32)
        total = total + (over_tensor(out.astype(BF), k).astype(F32) if k else out)
    token_grad = lax.dot_general(
        dispatch, total.astype(BF), (((0,), (0,)), ((), ())), preferred_element_type=F32
    ).astype(BF)

    for k in (1, 2, 4):
        route_part = route_part + over_tensor(route_part, k)
    route_grad = jnp.sum(jnp.where(mask, route_part[:, None], 0.0), axis=0)
    return token_grad, summed[:, :width], summed[:, width:], route_grad


def solution(mesh):
    return jax.shard_map(
        on_device,
        mesh=mesh,
        in_specs=(
            P("dp", "tensor"),
            P("dp", "tensor"),
            P(None, "tensor"),
            P(None, "tensor"),
            P("dp", None),
            P("dp", None),
        ),
        out_specs=(P("dp", "tensor"), P("dp", "tensor"), P("dp", "tensor"), P("dp")),
        check_vma=False,
    )
```

time: 405 us -> 184 us (0.45)
  waiting for transfers between devices: 333 us -> 58.8 us
  starting transfers between devices: 0.12 us -> 42.4 us
  blocking collectives: 17.2 us -> 0 us
  local copies, waits for them, and re-layouts: 2.07 us -> 17.2 us
  matrix products: 34.4 us -> 46.7 us
    reduce_scatter x2 -> x1, waiting for transfers between devices: 290 us -> 3.84 us  [on_device(): lax.psum_scatter(part, 'dp', scatter_dimension=0, tiled=True, axis_index_...]
    ppermute x0 -> x30, waiting for transfers between devices: none -> 55 us  [the longest x24 32.9 us: over_tensor(): return lax.ppermute(x, 'tensor', [(i, i ^ k) for i in range(n_tensor)])]
    all_gather x1 -> x0, waiting for transfers between devices: 42.7 us -> none  [on_device(): gathered = lax.all_gather(picked, 'tensor', axis=1, tiled=True)]
    ppermute x0 -> x30, starting transfers between devices: none -> 42.3 us  [the longest x24 37.5 us: over_tensor(): return lax.ppermute(x, 'tensor', [(i, i ^ k) for i in range(n_tensor)])]
    psum x1 -> x0, blocking collectives: 17.2 us -> none  [on_device(): lax.psum(jnp.sum(hidden_wide * cot_wide, axis=1), 'tensor')]
    dot_general x10 -> x22, matrix products: 34.4 us -> 46.7 us  [the longest x8 12.8 us: on_device(): out = lax.dot_general(gate_cot, wg, last, preferred_element_type=F32)]
    broadcast_in_dim x0 -> x18, local copies, waits for them, and re-layouts: none -> 7.56 us  [the longest x8 5.05 us: on_device(): far = lax.dynamic_update_index_in_dim(far, got, t ^ k, 0)]
    dynamic_update_slice x0 -> x16, local copies, waits for them, and re-layouts: none -> 6.52 us  [the longest x8 5.52 us: on_device(): near = lax.dynamic_update_index_in_dim(near, got, t ^ k, 0)]
  transfers between devices with their start and end apart: 3 -> 31, of which waited for: 3 -> 15; matrix products, arithmetic and copies ran while one was open for 4% -> 20% of each run, Pallas kernels for 0% -> 0%
where the time goes in v1:
time: 184 us; the launch traced here: 183 us
  waiting for transfers between devices  58.8 us (32%)
  matrix products  46.7 us (25%)
  starting transfers between devices  42.4 us (23%)
  local copies, waits for them, and re-layouts  17.2 us (9%)
  between operations  14.6 us (8%)
  other arithmetic  3.3 us (2%)
    ppermute x24, starting transfers between devices, over_tensor(): return lax.ppermute(x, 'tensor', [(i, i ^ k) for i in range(n_tensor)])  37.5 us
    ppermute x24, waiting for transfers between devices, over_tensor(): return lax.ppermute(x, 'tensor', [(i, i ^ k) for i in range(n_tensor)])  32.9 us
    ppermute x6, waiting for transfers between devices, over_dp(): return lax.ppermute(x, 'dp', [(i, i ^ k) for i in range(n_dp)])  22.1 us
    dot_general x8, matrix products, on_device(): out = lax.dot_general(gate_cot, wg, last, preferred_element_type=F32)  12.8 us
    dot_general x7, matrix products, on_device(): out = out + lax.dot_general(up_cot, wu, last, preferred_element_type=F32)  11.2 us
    dot_general x1, matrix products, on_device(): part = jnp.dot(left, right, preferred_element_type=F32).astype(BF)  8.99 us
    dynamic_update_slice x8, local copies, waits for them, and re-layouts, on_device(): near = lax.dynamic_update_index_in_dim(near, got, t ^ k, 0)  5.52 us
    dot_general x1, matrix products, on_device(): lax.dot_general(gathered, w_gate, first, preferred_element_type=F32)  5.48 us
  transfers between devices with their start and end apart: 31, of which 15 were waited for; matrix products, arithmetic and copies ran while one was open for 20% of the time, Pallas kernels for 0%

profile of v1, /device:TPU:2, one launch (start us, length us, event | category | flops | bytes accessed | tf_op | source)
XLA Modules:
  0.0 183.0 jit_solution(16313219905974619911)
XLA Ops:
  8.2 1.3 convolution_convert_fusion.2
  9.5 1.7 collective-permute-start
  11.2 2.9 %collective-permute-start.1 = (bf16[384,256]{0,1:T(8,128)(2,1)S(1)}, bf16[384,256]{0,1:T(8,128)(2,1)S(1)}, u32[]{:S(2)}, u32[]{:S(2)}) collective-permute-start(bf16[384,256]{0,1:T(8,128)(2,1)S(1)} %bitcast.59), channel_id=1, source_target_pairs={{0,2},{1,3},{2,0},{3,1},{4,6},{5,7},{6,4},{7,5},{8,10},{9,11},{10,... | collective-permute-start | bytes 589832 | tf_op jit(solution)/shard_map/ppermute | solution.py:23
  14.3 2.3 %collective-permute-start.3 = (bf16[384,256]{0,1:T(8,128)(2,1)S(1)}, bf16[384,256]{0,1:T(8,128)(2,1)S(1)}, u32[]{:S(2)}, u32[]{:S(2)}) collective-permute-start(bf16[384,256]{0,1:T(8,128)(2,1)S(1)} %bitcast.61), channel_id=1, source_target_pairs={{0,4},{1,5},{2,6},{3,7},{4,0},{5,1},{6,2},{7,3},{8,12},{9,13},{10,... | collective-permute-start | bytes 589832 | tf_op jit(solution)/shard_map/ppermute | solution.py:23
  17.4 3.2 %collective-permute-start.5 = (bf16[384,256]{0,1:T(8,128)(2,1)S(1)}, bf16[384,256]{0,1:T(8,128)(2,1)S(1)}, u32[]{:S(2)}, u32[]{:S(2)}) collective-permute-start(bf16[384,256]{0,1:T(8,128)(2,1)S(1)} %bitcast.63), channel_id=1, source_target_pairs={{0,6},{1,7},{2,4},{3,5},{4,2},{5,3},{6,0},{7,1},{8,14},{9,15},{10,... | collective-permute-start | bytes 589832 | tf_op jit(solution)/shard_map/ppermute | solution.py:23
  20.6 10.1 %collective-permute-done.1 = bf16[384,256]{0,1:T(8,128)(2,1)S(1)} collective-permute-done((bf16[384,256]{0,1:T(8,128)(2,1)S(1)}, bf16[384,256]{0,1:T(8,128)(2,1)S(1)}, u32[]{:S(2)}, u32[]{:S(2)}) %collective-permute-start.1) | collective-permute-done | bytes 196640 | tf_op jit(solution)/shard_map/ppermute | solution.py:23
  30.9 1.3 broadcast_in_dim.95
  33.8 4.7 %collective-permute-done.6 = bf16[384,256]{0,1:T(8,128)(2,1)S(1)} collective-permute-done((bf16[384,256]{0,1:T(8,128)(2,1)S(1)}, bf16[384,256]{0,1:T(8,128)(2,1)S(1)}, u32[]{:S(2)}, u32[]{:S(2)}) %collective-permute-start.6) | collective-permute-done | bytes 196640 | tf_op jit(solution)/shard_map/ppermute | solution.py:23
  43.4 5.5 %fusion.87 = f32[256,1024]{1,0:T(8,128)S(1)} fusion(bf16[3072,256]{1,0:T(8,128)(2,1)} %bitcast.10, bf16[3072,1024]{1,0:T(8,128)(2,1)} %param.8), kind=kOutput, calls=%fused_computation.126 | convolution fusion | flops 1610612736 | bytes 8912896 | tf_op jit(solution)/shard_map/dot_general | solution.py:53
  49.0 3.3 %multiply_convert_fusion = (bf16[256,1024]{1,0:T(8,128)(2,1)S(1)}, f32[256,1024]{1,0:T(8,128)S(1)}) fusion(f32[256,1024]{1,0:T(8,128)S(1)} %fusion.87, bf16[3072,256]{1,0:T(8,128)(2,1)} %bitcast.10, bf16[3072,1024]{1,0:T(8,128)(2,1)S(1)} %bitcast.56), kind=kOutput, calls=%fused_computation.46 | convolution fusion | flops 1612185600 | bytes 10485760 | tf_op jit(solution)/shard_map/dot_general | solution.py:54
  52.9 3.6 %collective-permute-done.27 = f32[256]{0:T(256)S(1)} collective-permute-done((f32[256]{0:T(256)S(1)}, f32[256]{0:T(256)S(1)}, u32[]{:S(2)}, u32[]{:S(2)}) %collective-permute-start.27) | collective-permute-done | bytes 1056 | tf_op jit(solution)/shard_map/ppermute | solution.py:23
  56.5 1.7 collective-permute-start.28
  58.2 3.4 %collective-permute-done.28 = f32[256]{0:T(256)S(1)} collective-permute-done((f32[256]{0:T(256)S(1)}, f32[256]{0:T(256)S(1)}, u32[]{:S(2)}, u32[]{:S(2)}) %collective-permute-start.28) | collective-permute-done | bytes 1056 | tf_op jit(solution)/shard_map/ppermute | solution.py:23
  61.6 1.2 collective-permute-start.29
  62.8 2.3 %collective-permute-done.29 = f32[256]{0:T(256)S(1)} collective-permute-done((f32[256]{0:T(256)S(1)}, f32[256]{0:T(256)S(1)}, u32[]{:S(2)}, u32[]{:S(2)}) %collective-permute-start.29) | collective-permute-done | bytes 1056 | tf_op jit(solution)/shard_map/ppermute | solution.py:23
  67.6 2.5 %collective-permute-start.25 = (bf16[256,2048]{1,0:T(8,128)(2,1)}, bf16[256,2048]{1,0:T(8,128)(2,1)}, u32[]{:S(2)}, u32[]{:S(2)}) collective-permute-start(bf16[256,2048]{1,0:T(8,128)(2,1)} %pad_maximum_fusion), channel_id=1, source_target_pairs={{0,16},{8,24},{16,0},{24,8},{32,48},{40,56},{48,32},{56,40},{64,80... | collective-permute-start | bytes 3145736 | tf_op jit(solution)/shard_map/ppermute | solution.py:26
  71.4 19.1 %collective-permute-done.15 = bf16[192,256]{0,1:T(8,128)(2,1)S(1)} collective-permute-done((bf16[192,256]{0,1:T(8,128)(2,1)S(1)}, bf16[192,256]{0,1:T(8,128)(2,1)S(1)}, u32[]{:S(2)}, u32[]{:S(2)}) %collective-permute-start.15) | collective-permute-done | bytes 98336 | tf_op jit(solution)/shard_map/ppermute | solution.py:26
  92.1 3.1 %collective-permute-start.18 = (bf16[192,256]{0,1:T(8,128)(2,1)S(1)}, bf16[192,256]{0,1:T(8,128)(2,1)S(1)}, u32[]{:S(2)}, u32[]{:S(2)}) collective-permute-start(bf16[192,256]{0,1:T(8,128)(2,1)S(1)} %collective-permute-done.15), channel_id=1, source_target_pairs={{0,3},{1,2},{2,1},{3,0},{4,7},{5,6},{6,5},{7,4},{8,11},{9,10},{10,... | collective-permute-start | bytes 294920 | tf_op jit(solution)/shard_map/ppermute | solution.py:23
  95.2 1.9 %collective-permute-start.19 = (bf16[192,256]{0,1:T(8,128)(2,1)S(1)}, bf16[192,256]{0,1:T(8,128)(2,1)}, u32[]{:S(2)}, u32[]{:S(2)}) collective-permute-start(bf16[192,256]{0,1:T(8,128)(2,1)S(1)} %collective-permute-done.15), channel_id=1, source_target_pairs={{0,4},{1,5},{2,6},{3,7},{4,0},{5,1},{6,2},{7,3},{8,12},{9,13},{10,... | collective-permute-start | bytes 294920 | tf_op jit(solution)/shard_map/ppermute | solution.py:23
  98.7 2.1 %collective-permute-start.21 = (bf16[192,256]{0,1:T(8,128)(2,1)S(1)}, bf16[192,256]{0,1:T(8,128)(2,1)}, u32[]{:S(2)}, u32[]{:S(2)}) collective-permute-start(bf16[192,256]{0,1:T(8,128)(2,1)S(1)} %collective-permute-done.15), channel_id=1, source_target_pairs={{0,6},{1,7},{2,4},{3,5},{4,2},{5,3},{6,0},{7,1},{8,14},{9,15},{10,... | collective-permute-start | bytes 294920 | tf_op jit(solution)/shard_map/ppermute | solution.py:23
  100.8 2.4 %collective-permute-start.22 = (bf16[192,256]{0,1:T(8,128)(2,1)S(1)}, bf16[192,256]{0,1:T(8,128)(2,1)}, u32[]{:S(2)}, u32[]{:S(2)}) collective-permute-start(bf16[192,256]{0,1:T(8,128)(2,1)S(1)} %collective-permute-done.15), channel_id=1, source_target_pairs={{0,7},{1,6},{2,5},{3,4},{4,3},{5,2},{6,1},{7,0},{8,15},{9,14},{10,... | collective-permute-start | bytes 294920 | tf_op jit(solution)/shard_map/ppermute | solution.py:23
  110.9 1.2 constant_dynamic-slice_fusion.1
  112.6 1.3 collective-permute-done.23
  115.6 9.0 %fusion.10 = bf16[768,2048]{1,0:T(8,128)(2,1)} fusion(bf16[256,2048]{1,0:T(8,128)(2,1)S(1)} %collective-permute-done.26, bf16[256,2048]{1,0:T(8,128)(2,1)} %collective-permute-done.25, bf16[256,2048]{1,0:T(8,128)(2,1)S(1)} %collective-permute-done.24, bf16[256,1024]{1,0:T(8,128)(2,1)S(1)} %get-tuple-element.6, bf16[256,1024]{1,0:T(8,128)(2,1)S(1)} %get-tuple-element.7, ...), kind=kOutput, calls=%fused_computation.10 | convolution fusion | flops 3250061312 | bytes 8912896 | tf_op jit(solution)/shard_map/dot_general | solution.py:83
  124.6 1.6 fusion.55
  126.2 1.6 fusion.22
  128.9 1.6 fusion.52
  130.5 1.6 fusion.23
  132.1 3.0 %collective-permute-start.8 = (bf16[256,384]{1,0:T(8,128)(2,1)S(1)}, bf16[256,384]{1,0:T(8,128)(2,1)S(1)}, u32[]{:S(2)}, u32[]{:S(2)}) collective-permute-start(bf16[256,384]{1,0:T(8,128)(2,1)S(1)} %fusion.23), channel_id=1, source_target_pairs={{0,2},{1,3},{2,0},{3,1},{4,6},{5,7},{6,4},{7,5},{8,10},{9,11},{10,... | collective-permute-start | bytes 589832 | tf_op jit(solution)/shard_map/ppermute | solution.py:23
  135.1 1.6 fusion.49
  136.7 1.6 fusion.24
  139.4 1.6 fusion.46
  141.0 1.6 fusion.25
  142.6 2.0 %collective-permute-start.10 = (bf16[256,384]{1,0:T(8,128)(2,1)S(1)}, bf16[256,384]{1,0:T(8,128)(2,1)S(1)}, u32[]{:S(2)}, u32[]{:S(2)}) collective-permute-start(bf16[256,384]{1,0:T(8,128)(2,1)S(1)} %fusion.25), channel_id=1, source_target_pairs={{0,4},{1,5},{2,6},{3,7},{4,0},{5,1},{6,2},{7,3},{8,12},{9,13},{10,... | collective-permute-start | bytes 589832 | tf_op jit(solution)/shard_map/ppermute | solution.py:23
  144.6 1.6 fusion.43
  146.2 1.6 fusion.26
  148.0 1.6 fusion.40
  149.6 1.6 fusion.37
  151.2 1.6 fusion.27
  152.8 1.6 fusion.28
  154.4 3.4 %collective-permute-start.12 = (bf16[256,384]{1,0:T(8,128)(2,1)S(1)}, bf16[256,384]{1,0:T(8,128)(2,1)}, u32[]{:S(2)}, u32[]{:S(2)}) collective-permute-start(bf16[256,384]{1,0:T(8,128)(2,1)S(1)} %fusion.27), channel_id=1, source_target_pairs={{0,6},{1,7},{2,4},{3,5},{4,2},{5,3},{6,0},{7,1},{8,14},{9,15},{10,... | collective-permute-start | bytes 589832 | tf_op jit(solution)/shard_map/ppermute | solution.py:23
  157.8 1.8 collective-permute-start.13
  159.6 1.6 fusion.58
  161.2 3.6 %collective-permute-done.12 = bf16[256,384]{1,0:T(8,128)(2,1)} collective-permute-done((bf16[256,384]{1,0:T(8,128)(2,1)S(1)}, bf16[256,384]{1,0:T(8,128)(2,1)}, u32[]{:S(2)}, u32[]{:S(2)}) %collective-permute-start.12) | collective-permute-done | bytes 196640 | tf_op jit(solution)/shard_map/ppermute | solution.py:23
  164.9 2.8 %collective-permute-done.13 = bf16[256,384]{1,0:T(8,128)(2,1)} collective-permute-done((bf16[256,384]{1,0:T(8,128)(2,1)S(1)}, bf16[256,384]{1,0:T(8,128)(2,1)}, u32[]{:S(2)}, u32[]{:S(2)}) %collective-permute-start.13) | collective-permute-done | bytes 196640 | tf_op jit(solution)/shard_map/ppermute | solution.py:23
  167.7 2.9 %convolution_convert_fusion.1 = bf16[512,384]{1,0:T(8,128)(2,1)} fusion(s32[512]{0:T(512)S(1)} %convert_select_fusion, bf16[256,384]{1,0:T(8,128)(2,1)} %collective-permute-done.13, bf16[256,384]{1,0:T(8,128)(2,1)} %collective-permute-done.12, bf16[256,384]{1,0:T(8,128)(2,1)S(1)} %collective-permute-done.11, ...), kind=kOutput, calls=%fused_computation.21 | convolution fusion | flops 303890432 | bytes 3475460 | tf_op jit(solution)/shard_map/dot_general | solution.py:97
  170.6 3.8 %reduce-scatter.2.cloned.1.call-done = bf16[96,2048]{1,0:T(8,128)(2,1)} async-done(((bf16[768,2048]{1,0:T(8,128)(2,1)}), bf16[96,2048]{1,0:T(8,128)(2,1)}) %reduce-scatter.2.cloned.1.call-update) | async-done | bytes 393232 | tf_op jit(solution)/shard_map/reduce_scatter | solution.py:85
  174.4 1.8 fusion.86
  (97 shorter events, 28.5 us)
Async XLA Ops:
  7.2 45.1 %copy-start = (bf16[512,1024]{1,0:T(8,128)(2,1)S(1)}, bf16[512,1024]{1,0:T(8,128)(2,1)}, u32[]{:S(2)}) copy-start(bf16[512,1024]{1,0:T(8,128)(2,1)} %param.7) | copy-start | bytes 3145732
  7.2 167.2 %reduce-scatter.2.cloned.1.call-start = ((), (), s32[]{:S(2)}) async-start(), calls=%async_computation.1 | async-start | bytes 3538944 | tf_op jit(solution)/shard_map/reduce_scatter | solution.py:85
  9.5 7.9 %collective-permute-start = (bf16[384,256]{0,1:T(8,128)(2,1)S(1)}, bf16[384,256]{0,1:T(8,128)(2,1)S(1)}, u32[]{:S(2)}, u32[]{:S(2)}) collective-permute-start(bf16[384,256]{0,1:T(8,128)(2,1)S(1)} %bitcast.58), channel_id=1, source_target_pairs={{0,1},{1,0},{2,3},{3,2},{4,5},{5,4},{6,7},{7,6},{8,9},{9,8},{10,11... | collective-permute-start | bytes 589832 | tf_op jit(solution)/shard_map/ppermute | solution.py:23
  11.2 19.5 %collective-permute-start.1 = (bf16[384,256]{0,1:T(8,128)(2,1)S(1)}, bf16[384,256]{0,1:T(8,128)(2,1)S(1)}, u32[]{:S(2)}, u32[]{:S(2)}) collective-permute-start(bf16[384,256]{0,1:T(8,128)(2,1)S(1)} %bitcast.59), channel_id=1, source_target_pairs={{0,2},{1,3},{2,0},{3,1},{4,6},{5,7},{6,4},{7,5},{8,10},{9,11},{10,... | collective-permute-start | bytes 589832 | tf_op jit(solution)/shard_map/ppermute | solution.py:23
  14.1 19.0 %collective-permute-start.2 = (bf16[384,256]{0,1:T(8,128)(2,1)S(1)}, bf16[384,256]{0,1:T(8,128)(2,1)S(1)}, u32[]{:S(2)}, u32[]{:S(2)}) collective-permute-start(bf16[384,256]{0,1:T(8,128)(2,1)S(1)} %bitcast.60), channel_id=1, source_target_pairs={{0,3},{1,2},{2,1},{3,0},{4,7},{5,6},{6,5},{7,4},{8,11},{9,10},{10,... | collective-permute-start | bytes 589832 | tf_op jit(solution)/shard_map/ppermute | solution.py:23
  14.3 19.0 %collective-permute-start.3 = (bf16[384,256]{0,1:T(8,128)(2,1)S(1)}, bf16[384,256]{0,1:T(8,128)(2,1)S(1)}, u32[]{:S(2)}, u32[]{:S(2)}) collective-permute-start(bf16[384,256]{0,1:T(8,128)(2,1)S(1)} %bitcast.61), channel_id=1, source_target_pairs={{0,4},{1,5},{2,6},{3,7},{4,0},{5,1},{6,2},{7,3},{8,12},{9,13},{10,... | collective-permute-start | bytes 589832 | tf_op jit(solution)/shard_map/ppermute | solution.py:23
  16.6 16.9 %collective-permute-start.4 = (bf16[384,256]{0,1:T(8,128)(2,1)S(1)}, bf16[384,256]{0,1:T(8,128)(2,1)S(1)}, u32[]{:S(2)}, u32[]{:S(2)}) collective-permute-start(bf16[384,256]{0,1:T(8,128)(2,1)S(1)} %bitcast.62), channel_id=1, source_target_pairs={{0,5},{1,4},{2,7},{3,6},{4,1},{5,0},{6,3},{7,2},{8,13},{9,12},{10,... | collective-permute-start | bytes 589832 | tf_op jit(solution)/shard_map/ppermute | solution.py:23
  17.4 16.2 %collective-permute-start.5 = (bf16[384,256]{0,1:T(8,128)(2,1)S(1)}, bf16[384,256]{0,1:T(8,128)(2,1)S(1)}, u32[]{:S(2)}, u32[]{:S(2)}) collective-permute-start(bf16[384,256]{0,1:T(8,128)(2,1)S(1)} %bitcast.63), channel_id=1, source_target_pairs={{0,6},{1,7},{2,4},{3,5},{4,2},{5,3},{6,0},{7,1},{8,14},{9,15},{10,... | collective-permute-start | bytes 589832 | tf_op jit(solution)/shard_map/ppermute | solution.py:23
  30.7 7.8 %collective-permute-start.6 = (bf16[384,256]{0,1:T(8,128)(2,1)S(1)}, bf16[384,256]{0,1:T(8,128)(2,1)S(1)}, u32[]{:S(2)}, u32[]{:S(2)}) collective-permute-start(bf16[384,256]{0,1:T(8,128)(2,1)S(1)} %bitcast.64), channel_id=1, source_target_pairs={{0,7},{1,6},{2,5},{3,4},{4,3},{5,2},{6,1},{7,0},{8,15},{9,14},{10,... | collective-permute-start | bytes 589832 | tf_op jit(solution)/shard_map/ppermute | solution.py:23
  42.7 6.2 %slice-start = ((s8[6291456]{0:T(1024)(128)(4,1)}), s8[4194304]{0:T(1024)(128)(4,1)S(1)}, s32[]{:S(2)}) async-start(s8[6291456]{0:T(1024)(128)(4,1)} %bitcast.55), calls=%async_computation.2 | async-start | bytes 8388608
  43.4 5.5 %slice-start.1 = ((s8[6291456]{0:T(1024)(128)(4,1)}), s8[2097152]{0:T(1024)(128)(4,1)S(1)}, s32[]{:S(2)}) async-start(s8[6291456]{0:T(1024)(128)(4,1)} %bitcast.55), calls=%async_computation.3 | async-start | bytes 4194304
  48.9 9.3 %copy-start.1 = (s32[512,2]{0,1:T(2,128)S(1)}, s32[512,2]{0,1:T(2,128)}, u32[]{:S(2)}) copy-start(s32[512,2]{0,1:T(2,128)} %param.10) | copy-start | bytes 12292
  48.9 9.2 %copy-start.2 = (s32[512,2]{0,1:T(2,128)S(1)}, s32[512,2]{0,1:T(2,128)}, u32[]{:S(2)}) copy-start(s32[512,2]{0,1:T(2,128)} %param.11) | copy-start | bytes 12292
  52.8 3.7 %collective-permute-start.27 = (f32[256]{0:T(256)S(1)}, f32[256]{0:T(256)S(1)}, u32[]{:S(2)}, u32[]{:S(2)}) collective-permute-start(f32[256]{0:T(256)S(1)} %get-tuple-element.16), channel_id=1, source_target_pairs={{0,1},{1,0},{2,3},{3,2},{4,5},{5,4},{6,7},{7,6},{8,9},{9,8},{10,11... | collective-permute-start | bytes 3080 | tf_op jit(solution)/shard_map/ppermute | solution.py:23
  56.5 5.1 %collective-permute-start.28 = (f32[256]{0:T(256)S(1)}, f32[256]{0:T(256)S(1)}, u32[]{:S(2)}, u32[]{:S(2)}) collective-permute-start(f32[256]{0:T(256)S(1)} %add.205), channel_id=1, source_target_pairs={{0,2},{1,3},{2,0},{3,1},{4,6},{5,7},{6,4},{7,5},{8,10},{9,11},{10,... | collective-permute-start | bytes 3080 | tf_op jit(solution)/shard_map/ppermute | solution.py:23
  61.6 3.6 %collective-permute-start.29 = (f32[256]{0:T(256)S(1)}, f32[256]{0:T(256)S(1)}, u32[]{:S(2)}, u32[]{:S(2)}) collective-permute-start(f32[256]{0:T(256)S(1)} %add.206), channel_id=1, source_target_pairs={{0,4},{1,5},{2,6},{3,7},{4,0},{5,1},{6,2},{7,3},{8,12},{9,13},{10,... | collective-permute-start | bytes 3080 | tf_op jit(solution)/shard_map/ppermute | solution.py:23
  67.6 42.4 %collective-permute-start.25 = (bf16[256,2048]{1,0:T(8,128)(2,1)}, bf16[256,2048]{1,0:T(8,128)(2,1)}, u32[]{:S(2)}, u32[]{:S(2)}) collective-permute-start(bf16[256,2048]{1,0:T(8,128)(2,1)} %pad_maximum_fusion), channel_id=1, source_target_pairs={{0,16},{8,24},{16,0},{24,8},{32,48},{40,56},{48,32},{56,40},{64,80... | collective-permute-start | bytes 3145736 | tf_op jit(solution)/shard_map/ppermute | solution.py:26
  70.2 20.2 %collective-permute-start.15 = (bf16[192,256]{0,1:T(8,128)(2,1)S(1)}, bf16[192,256]{0,1:T(8,128)(2,1)S(1)}, u32[]{:S(2)}, u32[]{:S(2)}) collective-permute-start(bf16[192,256]{0,1:T(8,128)(2,1)S(1)} %dynamic-slice_bitcast_fusion.2), channel_id=1, source_target_pairs={{0,16},{8,24},{16,0},{24,8},{32,48},{40,56},{48,32},{56,40},{64,80... | collective-permute-start | bytes 294920 | tf_op jit(solution)/shard_map/ppermute | solution.py:26
  90.4 6.7 %collective-permute-start.16 = (bf16[192,256]{0,1:T(8,128)(2,1)S(1)}, bf16[192,256]{0,1:T(8,128)(2,1)S(1)}, u32[]{:S(2)}, u32[]{:S(2)}) collective-permute-start(bf16[192,256]{0,1:T(8,128)(2,1)S(1)} %collective-permute-done.15), channel_id=1, source_target_pairs={{0,1},{1,0},{2,3},{3,2},{4,5},{5,4},{6,7},{7,6},{8,9},{9,8},{10,11... | collective-permute-start | bytes 294920 | tf_op jit(solution)/shard_map/ppermute | solution.py:23
  91.0 7.7 %collective-permute-start.17 = (bf16[192,256]{0,1:T(8,128)(2,1)S(1)}, bf16[192,256]{0,1:T(8,128)(2,1)S(1)}, u32[]{:S(2)}, u32[]{:S(2)}) collective-permute-start(bf16[192,256]{0,1:T(8,128)(2,1)S(1)} %collective-permute-done.15), channel_id=1, source_target_pairs={{0,2},{1,3},{2,0},{3,1},{4,6},{5,7},{6,4},{7,5},{8,10},{9,11},{10,... | collective-permute-start | bytes 294920 | tf_op jit(solution)/shard_map/ppermute | solution.py:23
  92.1 8.8 %collective-permute-start.18 = (bf16[192,256]{0,1:T(8,128)(2,1)S(1)}, bf16[192,256]{0,1:T(8,128)(2,1)S(1)}, u32[]{:S(2)}, u32[]{:S(2)}) collective-permute-start(bf16[192,256]{0,1:T(8,128)(2,1)S(1)} %collective-permute-done.15), channel_id=1, source_target_pairs={{0,3},{1,2},{2,1},{3,0},{4,7},{5,6},{6,5},{7,4},{8,11},{9,10},{10,... | collective-permute-start | bytes 294920 | tf_op jit(solution)/shard_map/ppermute | solution.py:23
  95.2 9.0 %collective-permute-start.19 = (bf16[192,256]{0,1:T(8,128)(2,1)S(1)}, bf16[192,256]{0,1:T(8,128)(2,1)}, u32[]{:S(2)}, u32[]{:S(2)}) collective-permute-start(bf16[192,256]{0,1:T(8,128)(2,1)S(1)} %collective-permute-done.15), channel_id=1, source_target_pairs={{0,4},{1,5},{2,6},{3,7},{4,0},{5,1},{6,2},{7,3},{8,12},{9,13},{10,... | collective-permute-start | bytes 294920 | tf_op jit(solution)/shard_map/ppermute | solution.py:23
  97.2 8.1 %collective-permute-start.20 = (bf16[192,256]{0,1:T(8,128)(2,1)S(1)}, bf16[192,256]{0,1:T(8,128)(2,1)}, u32[]{:S(2)}, u32[]{:S(2)}) collective-permute-start(bf16[192,256]{0,1:T(8,128)(2,1)S(1)} %collective-permute-done.15), channel_id=1, source_target_pairs={{0,5},{1,4},{2,7},{3,6},{4,1},{5,0},{6,3},{7,2},{8,13},{9,12},{10,... | collective-permute-start | bytes 294920 | tf_op jit(solution)/shard_map/ppermute | solution.py:23
  98.7 7.6 %collective-permute-start.21 = (bf16[192,256]{0,1:T(8,128)(2,1)S(1)}, bf16[192,256]{0,1:T(8,128)(2,1)}, u32[]{:S(2)}, u32[]{:S(2)}) collective-permute-start(bf16[192,256]{0,1:T(8,128)(2,1)S(1)} %collective-permute-done.15), channel_id=1, source_target_pairs={{0,6},{1,7},{2,4},{3,5},{4,2},{5,3},{6,0},{7,1},{8,14},{9,15},{10,... | collective-permute-start | bytes 294920 | tf_op jit(solution)/shard_map/ppermute | solution.py:23
  100.8 7.2 %collective-permute-start.22 = (bf16[192,256]{0,1:T(8,128)(2,1)S(1)}, bf16[192,256]{0,1:T(8,128)(2,1)}, u32[]{:S(2)}, u32[]{:S(2)}) collective-permute-start(bf16[192,256]{0,1:T(8,128)(2,1)S(1)} %collective-permute-done.15), channel_id=1, source_target_pairs={{0,7},{1,6},{2,5},{3,4},{4,3},{5,2},{6,1},{7,0},{8,15},{9,14},{10,... | collective-permute-start | bytes 294920 | tf_op jit(solution)/shard_map/ppermute | solution.py:23
  110.0 5.0 %collective-permute-start.24 = (bf16[256,2048]{1,0:T(8,128)(2,1)}, bf16[256,2048]{1,0:T(8,128)(2,1)S(1)}, u32[]{:S(2)}, u32[]{:S(2)}) collective-permute-start(bf16[256,2048]{1,0:T(8,128)(2,1)} %pad_maximum_fusion), channel_id=1, source_target_pairs={{0,8},{8,0},{16,24},{24,16},{32,40},{40,32},{48,56},{56,48},{64,72... | collective-permute-start | bytes 3145736 | tf_op jit(solution)/shard_map/ppermute | solution.py:26
  110.1 5.5 %collective-permute-start.26 = (bf16[256,2048]{1,0:T(8,128)(2,1)}, bf16[256,2048]{1,0:T(8,128)(2,1)S(1)}, u32[]{:S(2)}, u32[]{:S(2)}) collective-permute-start(bf16[256,2048]{1,0:T(8,128)(2,1)} %collective-permute-done.25), channel_id=1, source_target_pairs={{0,8},{8,0},{16,24},{24,16},{32,40},{40,32},{48,56},{56,48},{64,72... | collective-permute-start | bytes 3145736 | tf_op jit(solution)/shard_map/ppermute | solution.py:26
  110.7 3.1 %collective-permute-start.23 = (bf16[8,96,256]{2,1,0:T(8,128)(2,1)S(1)}, bf16[8,96,256]{2,1,0:T(8,128)(2,1)S(1)}, u32[]{:S(2)}, u32[]{:S(2)}) collective-permute-start(bf16[8,96,256]{2,1,0:T(8,128)(2,1)S(1)} %get-tuple-element.11), channel_id=1, source_target_pairs={{0,8},{8,0},{16,24},{24,16},{32,40},{40,32},{48,56},{56,48},{64,72... | collective-permute-start | bytes 1179656 | tf_op jit(solution)/shard_map/ppermute | solution.py:26
  112.1 2.9 %collective-permute-start.14 = (bf16[8,96,256]{2,1,0:T(8,128)(2,1)S(1)}, bf16[8,96,256]{2,1,0:T(8,128)(2,1)S(1)}, u32[]{:S(2)}, u32[]{:S(2)}) collective-permute-start(bf16[8,96,256]{2,1,0:T(8,128)(2,1)S(1)} %get-tuple-element.9), channel_id=1, source_target_pairs={{0,8},{8,0},{16,24},{24,16},{32,40},{40,32},{48,56},{56,48},{64,72... | collective-permute-start | bytes 1179656 | tf_op jit(solution)/shard_map/ppermute | solution.py:26
  127.8 26.6 %collective-permute-start.7 = (bf16[256,384]{1,0:T(8,128)(2,1)S(1)}, bf16[256,384]{1,0:T(8,128)(2,1)S(1)}, u32[]{:S(2)}, u32[]{:S(2)}) collective-permute-start(bf16[256,384]{1,0:T(8,128)(2,1)S(1)} %fusion.22), channel_id=1, source_target_pairs={{0,1},{1,0},{2,3},{3,2},{4,5},{5,4},{6,7},{7,6},{8,9},{9,8},{10,11... | collective-permute-start | bytes 589832 | tf_op jit(solution)/shard_map/ppermute | solution.py:23
  132.1 25.7 %collective-permute-start.8 = (bf16[256,384]{1,0:T(8,128)(2,1)S(1)}, bf16[256,384]{1,0:T(8,128)(2,1)S(1)}, u32[]{:S(2)}, u32[]{:S(2)}) collective-permute-start(bf16[256,384]{1,0:T(8,128)(2,1)S(1)} %fusion.23), channel_id=1, source_target_pairs={{0,2},{1,3},{2,0},{3,1},{4,6},{5,7},{6,4},{7,5},{8,10},{9,11},{10,... | collective-permute-start | bytes 589832 | tf_op jit(solution)/shard_map/ppermute | solution.py:23
  138.3 22.9 %collective-permute-start.9 = (bf16[256,384]{1,0:T(8,128)(2,1)S(1)}, bf16[256,384]{1,0:T(8,128)(2,1)S(1)}, u32[]{:S(2)}, u32[]{:S(2)}) collective-permute-start(bf16[256,384]{1,0:T(8,128)(2,1)S(1)} %fusion.24), channel_id=1, source_target_pairs={{0,3},{1,2},{2,1},{3,0},{4,7},{5,6},{6,5},{7,4},{8,11},{9,10},{10,... | collective-permute-start | bytes 589832 | tf_op jit(solution)/shard_map/ppermute | solution.py:23
  142.6 18.6 %collective-permute-start.10 = (bf16[256,384]{1,0:T(8,128)(2,1)S(1)}, bf16[256,384]{1,0:T(8,128)(2,1)S(1)}, u32[]{:S(2)}, u32[]{:S(2)}) collective-permute-start(bf16[256,384]{1,0:T(8,128)(2,1)S(1)} %fusion.25), channel_id=1, source_target_pairs={{0,4},{1,5},{2,6},{3,7},{4,0},{5,1},{6,2},{7,3},{8,12},{9,13},{10,... | collective-permute-start | bytes 589832 | tf_op jit(solution)/shard_map/ppermute | solution.py:23
  147.9 13.4 %collective-permute-start.11 = (bf16[256,384]{1,0:T(8,128)(2,1)S(1)}, bf16[256,384]{1,0:T(8,128)(2,1)S(1)}, u32[]{:S(2)}, u32[]{:S(2)}) collective-permute-start(bf16[256,384]{1,0:T(8,128)(2,1)S(1)} %fusion.26), channel_id=1, source_target_pairs={{0,5},{1,4},{2,7},{3,6},{4,1},{5,0},{6,3},{7,2},{8,13},{9,12},{10,... | collective-permute-start | bytes 589832 | tf_op jit(solution)/shard_map/ppermute | solution.py:23
  154.4 10.4 %collective-permute-start.12 = (bf16[256,384]{1,0:T(8,128)(2,1)S(1)}, bf16[256,384]{1,0:T(8,128)(2,1)}, u32[]{:S(2)}, u32[]{:S(2)}) collective-permute-start(bf16[256,384]{1,0:T(8,128)(2,1)S(1)} %fusion.27), channel_id=1, source_target_pairs={{0,6},{1,7},{2,4},{3,5},{4,2},{5,3},{6,0},{7,1},{8,14},{9,15},{10,... | collective-permute-start | bytes 589832 | tf_op jit(solution)/shard_map/ppermute | solution.py:23
  157.8 9.8 %collective-permute-start.13 = (bf16[256,384]{1,0:T(8,128)(2,1)S(1)}, bf16[256,384]{1,0:T(8,128)(2,1)}, u32[]{:S(2)}, u32[]{:S(2)}) collective-permute-start(bf16[256,384]{1,0:T(8,128)(2,1)S(1)} %fusion.28), channel_id=1, source_target_pairs={{0,7},{1,6},{2,5},{3,4},{4,3},{5,2},{6,1},{7,0},{8,15},{9,14},{10,... | collective-permute-start | bytes 589832 | tf_op jit(solution)/shard_map/ppermute | solution.py:23
Sparse Core Ops, SparseCore 0:
  124.7 49.6 reduce-scatter.1
